TPU v7x, 256 devices: a whole 4x4x8 slice. The times are simulated.
256 devices in a mesh: seq: 64 (over z, y_lo, x), tp: 4 (over y_hi, core).
Axes of the slice: x: 4, y: 4 (y_hi: 2, y_lo: 2; y = y_hi * 2 + y_lo), z: 8, core: 2. Of those that a mesh axis runs over, the one named last changes fastest.
Arguments:
- queries: bfloat16 [16384, 4096], P('seq', 'tp'), may hold values from -6 to 6
- keys: bfloat16 [16384, 4096], P('seq', 'tp'), may hold values from -6 to 6
- values: bfloat16 [16384, 4096], P('seq', 'tp'), may hold values from -6 to 6
- filter_spectrum: float32 [2, 64, 256, 4096], P(None, 'seq', None, 'tp'), may hold values from -6 to 6
- weight: bfloat16 [4096, 4096], P('tp', 'seq'), may hold values from -0.09375 to 0.09375
- cotangent: bfloat16 [16384, 4096], P('seq', 'tp'), may hold values from -6 to 6
Outputs:
- output: bfloat16 [16384, 4096], P('seq', 'tp')
- grad_queries: bfloat16 [16384, 4096], P('seq', 'tp')
- grad_keys: bfloat16 [16384, 4096], P('seq', 'tp')
- grad_values: bfloat16 [16384, 4096], P('seq', 'tp')
- grad_filter: float32 [2, 64, 256, 4096], P(None, 'seq', None, 'tp')
All inputs are finite; a program needn't handle non-finite values.
Results may differ from a plain program's by a relative error of at most 0.024.
Values may be sent and summed in bfloat16 or wider, within the bound.
A program may use at most 128 MiB of HBM per device.

v0:
```python
import math

import jax
import jax.numpy as jnp
from jax import lax
from jax.sharding import PartitionSpec as P


def build_tables(tok_rows, splits):
    first = jnp.arange(tok_rows, dtype=jnp.int32)
    angle_a = (
        2.0 * math.pi / tok_rows * (first[:, None] * first[None, :] % tok_rows).astype(jnp.float32)
    )
    cos_a = jnp.cos(angle_a)
    sin_a = jnp.sin(angle_a)
    forward_a = jnp.stack([jnp.stack([cos_a, sin_a], 0), jnp.stack([-sin_a, cos_a], 0)], 0).astype(
        jnp.bfloat16
    )
    inverse_a = jnp.stack([jnp.stack([cos_a, -sin_a], 0), jnp.stack([sin_a, cos_a], 0)], 0).astype(
        jnp.bfloat16
    )
    second = jnp.arange(splits, dtype=jnp.int32)
    angle_b = (
        2.0 * math.pi / splits * (second[:, None] * second[None, :] % splits).astype(jnp.float32)
    )
    cos_b = jnp.cos(angle_b)
    sin_b = jnp.sin(angle_b)
    forward_b = jnp.stack([cos_b, -sin_b], 0).astype(jnp.bfloat16)
    inverse_b = jnp.stack([cos_b, -sin_b], 1).astype(jnp.bfloat16)
    return (forward_b, forward_a, inverse_a, inverse_b)


def rotate(real_part, imag_part, phase_angle, direction):
    cosine = jnp.cos(phase_angle)
    sine_part = direction * jnp.sin(phase_angle)
    return jnp.stack(
        [real_part * cosine - imag_part * sine_part, imag_part * cosine + real_part * sine_part], 0
    )


def product(left, right):
    return jnp.stack(
        [left[0] * right[0] - left[1] * right[1], left[0] * right[1] + left[1] * right[0]], 0
    )


def forward_spectrum(signal, tables, seq_rank, devices):
    forward_b, forward_a, inverse_a, inverse_b = tables
    tok_rows = signal.shape[0]
    channels = signal.shape[1]
    length = tok_rows * devices
    block = tok_rows // devices
    mixed_part = jnp.einsum(
        "xjb,abc->xjac",
        forward_b,
        lax.all_to_all(
            signal.reshape(tok_rows, 1, channels), "seq", split_axis=0, concat_axis=1, tiled=True
        ),
        preferred_element_type=jnp.float32,
    )
    split_ids = jnp.arange(devices, dtype=jnp.int32)
    pos_ids = seq_rank * block + jnp.arange(block, dtype=jnp.int32)
    phase_angle = (
        2.0
        * math.pi
        / length
        * (split_ids[:, None] * pos_ids[None, :] % length).astype(jnp.float32)
    )
    turned = rotate(mixed_part[0], mixed_part[1], phase_angle[:, :, None], -1.0).astype(
        jnp.bfloat16
    )
    return jnp.einsum(
        "xyka,yjac->xjkc",
        forward_a,
        lax.all_to_all(turned, "seq", split_axis=1, concat_axis=2, tiled=True),
        preferred_element_type=jnp.float32,
    ).astype(jnp.bfloat16)


def inverse_signal(spectra, tables, seq_rank, devices):
    forward_b, forward_a, inverse_a, inverse_b = tables
    tok_rows = spectra.shape[2]
    channels = spectra.shape[3]
    length = tok_rows * devices
    mixed_part = jnp.einsum(
        "xyak,yjkc->xjac", inverse_a, spectra, preferred_element_type=jnp.float32
    )
    pos_ids = jnp.arange(tok_rows, dtype=jnp.int32)
    phase_angle = 2.0 * math.pi / length * (seq_rank * pos_ids % length).astype(jnp.float32)
    turned = rotate(mixed_part[0], mixed_part[1], phase_angle[None, :, None], 1.0).astype(
        jnp.bfloat16
    )
    values_out = jnp.einsum(
        "byj,yjac->bac",
        inverse_b,
        lax.all_to_all(turned, "seq", split_axis=2, concat_axis=1, tiled=True),
        preferred_element_type=jnp.float32,
    ) * (1.0 / length)
    pieces = values_out.astype(jnp.bfloat16)
    arranged = lax.all_to_all(pieces, "seq", split_axis=0, concat_axis=1, tiled=True)
    return arranged.reshape(tok_rows, channels)


def shards(queries, keys, values, filter_spectrum, weight, cotangent):
    seq_rank = lax.axis_index("seq")
    devices = lax.axis_size("seq")
    tok_rows = queries.shape[0]
    length = tok_rows * devices
    tables = build_tables(tok_rows, devices)
    mixed_input = (keys.astype(jnp.float32) * values.astype(jnp.float32)).astype(jnp.bfloat16)
    input_spectrum = forward_spectrum(mixed_input, tables, seq_rank, devices)
    filtered = product(input_spectrum.astype(jnp.float32), filter_spectrum).astype(jnp.bfloat16)
    convolved = inverse_signal(filtered, tables, seq_rank, devices)
    gated = (queries.astype(jnp.float32) * convolved.astype(jnp.float32)).astype(jnp.bfloat16)
    full_cot = lax.all_gather(cotangent, "tp", axis=1, tiled=True)
    full_weight = lax.all_gather(weight, "seq", axis=1, tiled=True)
    partial_out = jnp.dot(gated, full_weight, preferred_element_type=jnp.float32)
    grad_gated = lax.dot_general(
        full_cot, full_weight, (((1,), (1,)), ((), ())), preferred_element_type=jnp.float32
    )
    output = lax.psum_scatter(
        partial_out.astype(jnp.bfloat16), "tp", scatter_dimension=1, tiled=True
    )
    grad_queries = (grad_gated * convolved.astype(jnp.float32)).astype(jnp.bfloat16)
    grad_convolved = (grad_gated * queries.astype(jnp.float32)).astype(jnp.bfloat16)
    grad_spectrum = forward_spectrum(grad_convolved, tables, seq_rank, devices).astype(jnp.float32)
    spec_float = input_spectrum.astype(jnp.float32)
    conj_input = jnp.stack([spec_float[0], -spec_float[1]], 0)
    grad_filter = product(conj_input, grad_spectrum) * (1.0 / length)
    conj_filter = jnp.stack([filter_spectrum[0], -filter_spectrum[1]], 0)
    grad_filtered = product(conj_filter, grad_spectrum).astype(jnp.bfloat16)
    grad_mixed = inverse_signal(grad_filtered, tables, seq_rank, devices).astype(jnp.float32)
    grad_keys = (grad_mixed * values.astype(jnp.float32)).astype(jnp.bfloat16)
    grad_values = (grad_mixed * keys.astype(jnp.float32)).astype(jnp.bfloat16)
    return (output, grad_queries, grad_keys, grad_values, grad_filter)


def solution(mesh):
    in_specs = (
        P("seq", "tp"),
        P("seq", "tp"),
        P("seq", "tp"),
        P(None, "seq", None, "tp"),
        P("tp", "seq"),
        P("seq", "tp"),
    )
    out_specs = (
        P("seq", "tp"),
        P("seq", "tp"),
        P("seq", "tp"),
        P("seq", "tp"),
        P(None, "seq", None, "tp"),
    )
    return jax.shard_map(shards, mesh=mesh, in_specs=in_specs, out_specs=out_specs, check_vma=False)
```

profile of v0, /device:TPU:8, one launch (start us, length us, event | category | flops | bytes accessed | tf_op | source)
XLA Modules:
  0.0 599.5 jit_solution(15786565001018579238)
XLA Ops:
  7.2 0.7 all-gather.5.cloned.1.call-update
  7.9 0.7 all-gather.3.cloned.1.call-update
  8.6 1.4 fusion.31
  10.0 0.5 broadcast.508
  10.6 1.0 reduce.3
  11.6 1.1 reshape.658
  12.7 12.9 %all-to-all-start = ((bf16[64,2,2048]{2,1,0:T(2,128)(2,1)}), bf16[64,2,2048]{2,1,0:T(2,128)(2,1)S(1)}, u32[]{:S(2)}, u32[]{:S(2)}) async-start(bf16[64,2,2048]{2,1,0:T(2,128)(2,1)} %reshape.658), calls=%async_computation | async-start | bytes 1048576 | tf_op jit(solution)/shard_map/all_to_all | solution.py:56
  25.7 20.9 %all-gather.5.cloned.1.call-done = bf16[256,4096]{1,0:T(8,128)(2,1)} async-done(((bf16[256,1024]{1,0:T(8,128)(2,1)}), bf16[256,4096]{1,0:T(8,128)(2,1)}) %all-gather.5.cloned.1.call-update) | async-done | bytes 2097168 | tf_op jit(solution)/shard_map/all_gather | solution.py:115
  46.6 309.9 %all-gather.3.cloned.1.call-done = bf16[1024,4096]{0,1:T(8,128)(2,1)} async-done(((bf16[1024,64]{0,1:T(8,128)(2,1)}), bf16[1024,4096]{0,1:T(8,128)(2,1)}) %all-gather.3.cloned.1.call-update) | async-done | bytes 8388624 | tf_op jit(solution)/shard_map/all_gather | solution.py:116
  356.5 6.3 %fusion.82 = f32[256,1024]{1,0:T(8,128)S(1)} fusion(bf16[256,4096]{1,0:T(8,128)(2,1)} %all-gather.5.cloned.1.call-done, bf16[1024,4096]{0,1:T(8,128)(2,1)} %all-gather.3.cloned.1.call-done), kind=kOutput, calls=%fused_computation.152 | convolution fusion | flops 2147483648 | bytes 11534336 | tf_op jit(solution)/shard_map/dot_general | solution.py:118
  362.8 1.0 copy-done.1
  364.0 1.0 reduce.2
  365.0 1.1 reshape.660
  366.1 14.9 %all-to-all-start.4 = ((bf16[64,2,2048]{2,1,0:T(2,128)(2,1)}), bf16[64,2,2048]{2,1,0:T(2,128)(2,1)}, u32[]{:S(2)}, u32[]{:S(2)}) async-start(bf16[64,2,2048]{2,1,0:T(2,128)(2,1)} %reshape.660), calls=%async_computation.5 | async-start | bytes 1048576 | tf_op jit(solution)/shard_map/all_to_all | solution.py:56
  381.3 0.5 reshape.659
  381.9 3.1 reduce
  385.2 0.5 fusion.36
  385.7 8.8 %all-to-all-done.4 = bf16[64,2,2048]{2,1,0:T(2,128)(2,1)} async-done(((bf16[64,2,2048]{2,1,0:T(2,128)(2,1)}), bf16[64,2,2048]{2,1,0:T(2,128)(2,1)}, u32[]{:S(2)}, u32[]{:S(2)}) %all-to-all-start.4) | async-done | bytes 524320 | tf_op jit(solution)/shard_map/all_to_all | solution.py:56
  394.4 3.6 reshape.661
  398.1 3.8 reduce.1
  401.9 1.2 all_to_all.81
  403.2 0.5 fusion.34
  403.7 0.8 subtract_convert_fusion.1
  404.6 1.8 copy.93
  406.4 6.0 all-to-all-start.5
  412.5 1.8 copy.79
  414.3 16.1 %all-to-all-done.5 = bf16[2,64,4,1024]{3,2,0,1:T(4,128)(2,1)S(1)} async-done(((bf16[2,64,4,1024]{3,2,0,1:T(4,128)(2,1)}), bf16[2,64,4,1024]{3,2,0,1:T(4,128)(2,1)S(1)}, u32[]{:S(2)}, u32[]{:S(2)}) %all-to-all-start.5) | async-done | bytes 1048608 | tf_op jit(solution)/shard_map/all_to_all | solution.py:75
  430.4 6.9 %all-to-all-start.1 = ((bf16[2,64,4,1024]{3,2,0,1:T(4,128)(2,1)}), bf16[2,64,4,1024]{3,2,0,1:T(4,128)(2,1)}, u32[]{:S(2)}, u32[]{:S(2)}) async-start(bf16[2,64,4,1024]{3,2,0,1:T(4,128)(2,1)} %copy.79), calls=%async_computation.1 | async-start | bytes 2097152 | tf_op jit(solution)/shard_map/all_to_all | solution.py:75
  437.4 2.7 fusion.81
  440.4 1.6 copy.114
  442.1 1.0 fusion.51
  443.1 1.1 negate_convert_fusion
  444.2 0.9 fusion.43
  445.1 2.1 copy.94
  447.2 2.4 copy.95
  449.6 10.4 %all-to-all-done.1 = bf16[2,64,4,1024]{3,2,0,1:T(4,128)(2,1)} async-done(((bf16[2,64,4,1024]{3,2,0,1:T(4,128)(2,1)}), bf16[2,64,4,1024]{3,2,0,1:T(4,128)(2,1)}, u32[]{:S(2)}, u32[]{:S(2)}) %all-to-all-start.1) | async-done | bytes 1048608 | tf_op jit(solution)/shard_map/all_to_all | solution.py:75
  460.0 3.3 copy.80
  463.3 3.7 copy.81
  466.9 1.8 convert_bitcast_fusion
  468.8 0.7 convert_bitcast_fusion.1
  469.5 0.5 fusion.28
  470.0 1.4 multiply_subtract_fusion
  471.4 0.7 convolution_bitcast_fusion.1
  472.2 0.7 convolution_bitcast_fusion
  472.9 1.4 subtract_convert_fusion
  474.4 2.2 copy.88
  476.6 6.7 %all-to-all-start.2 = ((bf16[2,1,256,1024]{3,0,1,2:T(2,128)(2,1)}), bf16[2,1,256,1024]{3,0,1,2:T(2,128)(2,1)S(1)}, u32[]{:S(2)}, u32[]{:S(2)}) async-start(bf16[2,1,256,1024]{3,0,1,2:T(2,128)(2,1)} %copy.88), calls=%async_computation.2 | async-start | bytes 2097152 | tf_op jit(solution)/shard_map/all_to_all | solution.py:96
  483.7 23.5 %all-to-all-done.2 = bf16[2,1,256,1024]{3,0,1,2:T(2,128)(2,1)S(1)} async-done(((bf16[2,1,256,1024]{3,0,1,2:T(2,128)(2,1)}), bf16[2,1,256,1024]{3,0,1,2:T(2,128)(2,1)S(1)}, u32[]{:S(2)}, u32[]{:S(2)}) %all-to-all-start.2) | async-done | bytes 1048608 | tf_op jit(solution)/shard_map/all_to_all | solution.py:96
  507.2 1.3 fusion.4
  508.5 0.4 copy.90
  508.9 21.0 %all_to_all.96 = bf16[64,4,1024]{2,1,0:T(4,128)(2,1)S(1)} all-to-all(bf16[64,4,1024]{2,1,0:T(4,128)(2,1)S(1)} %copy.90), channel_id=1, replica_groups=mesh['seq'=64,'tp'=4] {'seq'}, dimensions={0} | all-to-all | bytes 1048576 | tf_op jit(solution)/shard_map/all_to_all | solution.py:100
  530.0 7.7 %convolution_convert_fusion = bf16[256,4096]{1,0:T(8,128)(2,1)} fusion(bf16[1024,4096]{0,1:T(8,128)(2,1)} %all-gather.3.cloned.1.call-done, f32[256,1024]{1,0:T(8,128)S(1)} %reshape.638, bf16[256,1024]{1,0:T(8,128)(2,1)} %param.6), kind=kOutput, calls=%fused_computation | convolution fusion | flops 2149318656 | bytes 12058624 | tf_op jit(solution)/shard_map/dot_general | solution.py:117
  537.7 1.0 copy-done.8
  538.9 1.1 copy.101
  540.0 25.9 %all_to_all.97 = bf16[2,1,256,1024]{3,0,1,2:T(2,128)(2,1)S(1)} all-to-all(bf16[2,1,256,1024]{3,0,1,2:T(2,128)(2,1)S(1)} %copy.101), channel_id=1, replica_groups=mesh['seq'=64,'tp'=4] {'seq'}, dimensions={2} | all-to-all | bytes 2097152 | tf_op jit(solution)/shard_map/all_to_all | solution.py:96
  565.9 1.3 fusion.5
  567.2 1.2 copy.103
  568.4 6.9 %all-to-all-start.7 = ((bf16[64,4,1024]{2,1,0:T(4,128)(2,1)}), bf16[64,4,1024]{2,1,0:T(4,128)(2,1)}, u32[]{:S(2)}, u32[]{:S(2)}) async-start(bf16[64,4,1024]{2,1,0:T(4,128)(2,1)} %copy.103), calls=%async_computation.8 | async-start | bytes 1048576 | tf_op jit(solution)/shard_map/all_to_all | solution.py:100
  575.4 1.4 maximum_multiply_fusion
  576.7 1.8 copy.104
  578.5 10.4 %all-to-all-done.7 = bf16[64,4,1024]{2,1,0:T(4,128)(2,1)} async-done(((bf16[64,4,1024]{2,1,0:T(4,128)(2,1)}), bf16[64,4,1024]{2,1,0:T(4,128)(2,1)}, u32[]{:S(2)}, u32[]{:S(2)}) %all-to-all-start.7) | async-done | bytes 524320 | tf_op jit(solution)/shard_map/all_to_all | solution.py:100
  588.9 1.1 reshape.639
  590.1 0.9 multiply_convert_fusion
  591.5 1.3 fusion.8
  (41 shorter events, 2.5 us)
Async XLA Ops:
  7.2 39.4 %all-gather.5.cloned.1.call-start = ((), (), s32[]{:S(2)}) async-start(), calls=%async_computation.11 | async-start | bytes 2621440 | tf_op jit(solution)/shard_map/all_gather | solution.py:115
  7.9 348.6 %all-gather.3.cloned.1.call-start = ((), (), s32[]{:S(2)}) async-start(), calls=%async_computation.9 | async-start | bytes 8519680 | tf_op jit(solution)/shard_map/all_gather | solution.py:116
  12.7 353.4 %all-to-all-start = ((bf16[64,2,2048]{2,1,0:T(2,128)(2,1)}), bf16[64,2,2048]{2,1,0:T(2,128)(2,1)S(1)}, u32[]{:S(2)}, u32[]{:S(2)}) async-start(bf16[64,2,2048]{2,1,0:T(2,128)(2,1)} %reshape.658), calls=%async_computation | async-start | bytes 1048576 | tf_op jit(solution)/shard_map/all_to_all | solution.py:56
  25.7 338.1 %copy-start.9 = (bf16[256,1024]{1,0:T(8,128)(2,1)S(1)}, bf16[256,1024]{1,0:T(8,128)(2,1)}, u32[]{:S(2)}) copy-start(bf16[256,1024]{1,0:T(8,128)(2,1)} %param.6) | copy-start | bytes 1572868
  362.8 1.0 copy-start.1
  366.1 28.3 %all-to-all-start.4 = ((bf16[64,2,2048]{2,1,0:T(2,128)(2,1)}), bf16[64,2,2048]{2,1,0:T(2,128)(2,1)}, u32[]{:S(2)}, u32[]{:S(2)}) async-start(bf16[64,2,2048]{2,1,0:T(2,128)(2,1)} %reshape.660), calls=%async_computation.5 | async-start | bytes 1048576 | tf_op jit(solution)/shard_map/all_to_all | solution.py:56
  406.4 24.1 %all-to-all-start.5 = ((bf16[2,64,4,1024]{3,2,0,1:T(4,128)(2,1)}), bf16[2,64,4,1024]{3,2,0,1:T(4,128)(2,1)S(1)}, u32[]{:S(2)}, u32[]{:S(2)}) async-start(bf16[2,64,4,1024]{3,2,0,1:T(4,128)(2,1)} %copy.93), calls=%async_computation.6 | async-start | bytes 2097152 | tf_op jit(solution)/shard_map/all_to_all | solution.py:75
  430.4 29.5 %all-to-all-start.1 = ((bf16[2,64,4,1024]{3,2,0,1:T(4,128)(2,1)}), bf16[2,64,4,1024]{3,2,0,1:T(4,128)(2,1)}, u32[]{:S(2)}, u32[]{:S(2)}) async-start(bf16[2,64,4,1024]{3,2,0,1:T(4,128)(2,1)} %copy.79), calls=%async_computation.1 | async-start | bytes 2097152 | tf_op jit(solution)/shard_map/all_to_all | solution.py:75
  466.9 1.8 copy-start
  466.9 1.8 copy-start.5
  470.0 1.4 copy-start.10
  470.0 1.4 copy-start.11
  476.6 30.6 %all-to-all-start.2 = ((bf16[2,1,256,1024]{3,0,1,2:T(2,128)(2,1)}), bf16[2,1,256,1024]{3,0,1,2:T(2,128)(2,1)S(1)}, u32[]{:S(2)}, u32[]{:S(2)}) async-start(bf16[2,1,256,1024]{3,0,1,2:T(2,128)(2,1)} %copy.88), calls=%async_computation.2 | async-start | bytes 2097152 | tf_op jit(solution)/shard_map/all_to_all | solution.py:96
  483.3 109.4 %reduce-scatter.2.cloned.1.call-start = ((), (), s32[]{:S(2)}) async-start(), calls=%async_computation.10 | async-start | bytes 2621440 | tf_op jit(solution)/shard_map/reduce_scatter | solution.py:121
  530.0 7.7 %copy-start.3 = (f32[256,1024]{1,0:T(8,128)}, f32[256,1024]{1,0:T(8,128)S(1)}, u32[]{:S(2)}) copy-start(f32[256,1024]{1,0:T(8,128)S(1)} %reshape.638) | copy-start | bytes 3145732
  537.7 1.0 copy-start.8
  568.4 20.5 %all-to-all-start.7 = ((bf16[64,4,1024]{2,1,0:T(4,128)(2,1)}), bf16[64,4,1024]{2,1,0:T(4,128)(2,1)}, u32[]{:S(2)}, u32[]{:S(2)}) async-start(bf16[64,4,1024]{2,1,0:T(4,128)(2,1)} %copy.103), calls=%async_computation.8 | async-start | bytes 1048576 | tf_op jit(solution)/shard_map/all_to_all | solution.py:100
  576.7 13.3 %copy-start.2 = (f32[256,1024]{1,0:T(8,128)S(1)}, f32[256,1024]{1,0:T(8,128)}, u32[]{:S(2)}) copy-start(f32[256,1024]{1,0:T(8,128)} %copy-done.1) | copy-start | bytes 3145732
  578.5 11.5 %copy-start.4 = (f32[256,1024]{1,0:T(8,128)S(1)}, f32[256,1024]{1,0:T(8,128)}, u32[]{:S(2)}) copy-start(f32[256,1024]{1,0:T(8,128)} %copy-done.3) | copy-start | bytes 3145732
  590.1 1.0 copy-start.6
  590.1 1.4 copy-start.7
Sparse Core Ops, SparseCore 0:
  9.8 36.7 all-gather.4
  48.4 308.0 all-gather.2
  537.9 38.8 reduce-scatter.1
where the time goes:
time: 605 us; the launch traced here: 600 us
  waiting for transfers between devices  401 us (66%)
  starting transfers between devices  54.8 us (9%)
  blocking collectives  46.9 us (8%)
  local copies, waits for them, and re-layouts  38.4 us (6%)
  other arithmetic  22.1 us (4%)
  matrix products  21.6 us (4%)
  between operations  14.3 us (2%)
    all_gather x1, waiting for transfers between devices, shards(): full_weight = lax.all_gather(weight, 'seq', axis=1, tiled=True)  310 us
    all_to_all x2, starting transfers between devices, forward_spectrum(): lax.all_to_all(signal.reshape(tok_rows, 1, channels), 'seq', split_axis=0...  27.8 us
    all_to_all x2, waiting for transfers between devices, forward_spectrum(): lax.all_to_all(turned, 'seq', split_axis=1, concat_axis=2, tiled=True)  26.5 us
    all_to_all x1, blocking collectives, inverse_signal(): lax.all_to_all(turned, 'seq', split_axis=2, concat_axis=1, tiled=True)  25.9 us
    all_to_all x1, waiting for transfers between devices, inverse_signal(): lax.all_to_all(turned, 'seq', split_axis=2, concat_axis=1, tiled=True)  23.5 us
    all_to_all x1, blocking collectives, inverse_signal(): lax.all_to_all(pieces, 'seq', split_axis=0, concat_axis=1, tiled=True)  21 us
    all_gather x1, waiting for transfers between devices, shards(): full_cot = lax.all_gather(cotangent, 'tp', axis=1, tiled=True)  20.9 us
    all_to_all x2, starting transfers between devices, forward_spectrum(): lax.all_to_all(turned, 'seq', split_axis=1, concat_axis=2, tiled=True)  12.9 us
  transfers between devices with their start and end apart: 9, of which 7 were waited for; matrix products, arithmetic and copies ran while one was open for 7% of the time, Pallas kernels for 0%

commit v1 on v0

v1 whole, which is shorter than its diff:
```python
import math

import jax
import jax.numpy as jnp
import numpy as np
from jax import lax
from jax.experimental import pallas as pl
from jax.experimental.pallas import tpu as pltpu
from jax.sharding import PartitionSpec as P

MESH = pl.DeviceIdType.MESH
BF = jnp.bfloat16
F32 = jnp.float32

NZ, NY, NX = 8, 2, 4
NS = NZ * NY * NX
NR = NY * NX
TOK = 256
CH = 1024
OWN = CH // NS
FEAT = 64
LENGTH = TOK * NS
ROWS = NS * OWN


def tables():
    b = np.arange(NS)
    ang = 2.0 * np.pi / NS * (b[:, None] * b[None, :] % NS)
    wb = np.concatenate([np.cos(ang), -np.sin(ang)], 0)
    wbi = np.concatenate([np.cos(ang), -np.sin(ang)], 1)
    a = np.arange(TOK)
    ang = 2.0 * np.pi / TOK * (a[:, None] * a[None, :] % TOK)
    c, s = np.cos(ang), np.sin(ang)
    fwd = np.block([[c, -s], [s, c]])
    inv = np.block([[c, s], [-s, c]])
    ang = 2.0 * np.pi / LENGTH * (b[:, None] * a[None, :] % LENGTH)
    low = [jnp.asarray(t.astype(np.float32)).astype(BF) for t in (wb, wbi, fwd, inv)]
    return (*low, jnp.asarray(np.cos(ang).astype(np.float32)), jnp.asarray(np.sin(ang).astype(np.float32)))


def kernel(
    keys, values, queries, cot, filt, wt, wb, wbi, dfa, dia, cosr, sinr,
    out, gq, gk, gv, gf,
    kv, vv, qv, cotf, fv, wall, xs, xr, fs, fr, spec, gspec, s32, t32, cs, cr, gcs, gcr, gfs, gfr, gms, gmr,
    conv, gg, part, prec, osum, orec, stage,
    lsem, osem, a2s, a2r, zs, zr, ws, wr, ts, tr,
):
    s = lax.axis_index("seq")
    t = lax.axis_index("tp")
    z, r = s // NR, lax.rem(s, NR)
    yl, x = r // NX, lax.rem(r, NX)
    h, core = t // 2, lax.rem(t, 2)
    sib = h * 2 + (1 - core)
    far = (1 - h) * 2 + core

    def load(i, src, dst):
        return pltpu.make_async_copy(src, dst, lsem.at[i])

    loads = [
        load(0, wt, wall.at[z, r]),
        load(1, keys, kv),
        load(2, values, vv),
        load(3, cot, cotf.at[t]),
        load(4, filt, fv),
        load(5, queries, qv),
    ]
    for one in loads:
        one.start()

    barrier = pltpu.get_barrier_semaphore()

    def greet(i, carry):
        pl.semaphore_signal(barrier, inc=1, device_id={"seq": lax.rem(s + i, NS)}, device_id_type=MESH)
        return carry

    lax.fori_loop(1, NS, greet, 0)
    for i in range(1, 4):
        pl.semaphore_signal(barrier, inc=1, device_id={"tp": lax.rem(t + i, 4)}, device_id_type=MESH)

    def rows_out(val, dst, at, c):
        moved = val.T.astype(BF).reshape(8, OWN, TOK)
        if at is None:
            dst[pl.ds(8 * c, 8)] = moved
        else:
            dst[pl.ds(8 * c, 8), at] = moved

    def lanes(c):
        return pl.ds(pl.multiple_of(c * 128, 128), 128)

    def loop(n, body):
        def step(i, carry):
            body(i)
            return carry

        lax.fori_loop(0, n, step, 0)

    loads[1].wait()
    loads[2].wait()

    def mix(c):
        at = lanes(c)
        rows_out(kv[:, at].astype(F32) * vv[:, at].astype(F32), xs, None, c)

    loop(8, mix)
    loads[0].wait()
    loads[3].wait()

    pl.semaphore_wait(barrier, NS - 1 + 3)

    def remote(src, dst, ss, rs, **to):
        return pltpu.make_async_remote_copy(
            src_ref=src, dst_ref=dst, send_sem=ss, recv_sem=rs, device_id=to, device_id_type=MESH
        )

    def send_all(i, src, dst):
        def one(k, carry):
            d = lax.rem(s + k, NS)
            remote(src.at[d], dst.at[s], a2s.at[i], a2r.at[i], seq=d).start()
            return carry

        lax.fori_loop(1, NS, one, 0)
        dst[s] = src[s]

    def wait_all(i, src, dst):
        remote(src.at[pl.ds(0, NS - 1)], dst.at[pl.ds(0, NS - 1)], a2s.at[i], a2r.at[i], seq=s).wait_recv()

    def zdev(k):
        return lax.rem(z + k + NZ, NZ)

    def zcopy(k, way):
        src = wall.at[zdev(-k * way), r]
        if k == 3:
            src = wall.at[zdev(-k * way), r, pl.ds(0 if way > 0 else FEAT // 2, FEAT // 2)]
        i = 0 if way > 0 else 1
        return remote(src, src, zs.at[i, k], zr.at[i, k], seq=zdev(way) * NR + r)

    def zwait(k):
        for i, way in ((0, 1), (1, -1)):
            src = wall.at[zdev(-(k + 1) * way), r]
            if k == 3:
                src = wall.at[zdev(-(k + 1) * way), r, pl.ds(0 if way > 0 else FEAT // 2, FEAT // 2)]
            remote(src, src, zs.at[i, k], zr.at[i, k], seq=zdev(way) * NR + r).wait_recv()

    def zstart(k):
        zcopy(k, 1).start()
        zcopy(k, -1).start()

    def rx(k):
        return yl * NX + lax.rem(x + k + NX, NX)

    def rp(k):
        return (1 - yl) * NX + lax.rem(x + k + NX, NX)

    low, high = (0, 4), (4, 4)

    def rows(part_of, ri):
        return wall.at[pl.ds(part_of[0], part_of[1]), ri]

    plan = {
        0: (low, rx(0), rp(0), rp(0)),
        1: (high, rx(0), rx(-1), rx(1)),
        2: (high, rx(0), rx(1), rx(-1)),
        3: (high, rx(0), rp(0), rp(0)),
        4: (low, rx(0), rx(-1), rx(1)),
        5: (low, rx(0), rx(1), rx(-1)),
        6: (low, rp(0), rp(-1), rx(1)),
        7: (low, rp(0), rp(1), rx(-1)),
        8: ((4, 2), rx(-1), rx(-2), rx(1)),
        9: ((6, 2), rx(1), rx(2), rx(-1)),
        10: (high, rx(-1), rp(-1), rp(0)),
        11: (high, rx(1), rp(1), rp(0)),
        12: (high, rx(2), rp(2), rp(0)),
        13: ((0, 2), rx(-1), rx(-2), rx(1)),
        14: ((2, 2), rx(1), rx(2), rx(-1)),
        15: ((0, 2), rp(-1), rp(-2), rx(1)),
        16: ((2, 2), rp(1), rp(2), rx(-1)),
    }

    def wcopy(i, back=False):
        half, sent, received, to = plan[i]
        ref = rows(half, received if back else sent)
        return remote(ref, ref, ws.at[i], wr.at[i], seq=z * NR + to)

    def wstart(*which):
        for i in which:
            wcopy(i).start()

    def wwait(*which):
        for i in which:
            wcopy(i, True).wait_recv()

    def forward(src, dst):
        def widen(m):
            wide = src[pl.ds(8 * m, 8)].reshape(128, TOK).astype(F32)
            for lane in range(2):
                s32[lane, pl.ds(128 * m, 128)] = wide[:, 128 * lane : 128 * lane + 128]

        loop(8, widen)
        for c in range(OWN):
            at = pl.ds(c, NS, stride=OWN)
            taken = jnp.concatenate([s32[lane, at, :] for lane in range(2)], 1).astype(BF)
            y = jnp.dot(wb[...], taken, preferred_element_type=F32)
            re, im = y[:NS], y[NS:]
            tre = re * cosr[...] + im * sinr[...]
            tim = im * cosr[...] - re * sinr[...]
            for lane in range(2):
                t32[lane, at, :] = tre[:, 128 * lane : 128 * lane + 128]
                t32[2 + lane, at, :] = tim[:, 128 * lane : 128 * lane + 128]

        def second(m):
            at = pl.ds(128 * m, 128)
            left = jnp.concatenate([t32[lane, at] for lane in range(4)], 1).astype(BF)
            dst[at] = jnp.dot(left, dfa[...], preferred_element_type=F32).astype(BF)

        loop(8, second)

    def filter_at(m):
        at = pl.ds(8 * m, 8)
        return fr[at, 0].reshape(128, TOK).astype(F32), fr[at, 1].reshape(128, TOK).astype(F32)

    def inverse(src, conj, dst):
        def first(m):
            at = pl.ds(128 * m, 128)
            sre, sim = src[at, 0:TOK].astype(F32), src[at, TOK:].astype(F32)
            fre, fim = filter_at(m)
            if conj:
                fim = -fim
            y = jnp.concatenate([sre * fre - sim * fim, sre * fim + sim * fre], 1).astype(BF)
            o = jnp.dot(y, dia[...], preferred_element_type=F32)
            for lane in range(4):
                t32[lane, at] = o[:, 128 * lane : 128 * lane + 128]

        loop(8, first)
        for c in range(OWN):
            at = pl.ds(c, NS, stride=OWN)
            re = jnp.concatenate([t32[lane, at, :] for lane in range(2)], 1)
            im = jnp.concatenate([t32[2 + lane, at, :] for lane in range(2)], 1)
            tre = re * cosr[...] - im * sinr[...]
            tim = im * cosr[...] + re * sinr[...]
            both = jnp.concatenate([tre, tim], 0).astype(BF)
            o = jnp.dot(wbi[...], both, preferred_element_type=F32) * (1.0 / LENGTH)
            for lane in range(2):
                s32[lane, at, :] = o[:, 128 * lane : 128 * lane + 128]

        def narrow(m):
            wide = jnp.concatenate([s32[lane, pl.ds(128 * m, 128)] for lane in range(2)], 1)
            dst[pl.ds(8 * m, 8)] = wide.astype(BF).reshape(8, OWN, TOK)

        loop(8, narrow)

    def back_at(src, c):
        return src[pl.ds(8 * c, 8)].reshape(128, TOK).astype(F32).T

    zstart(0)
    cot_sib = remote(cotf.at[t], cotf.at[t], ts.at[0], tr.at[0], tp=sib)
    cot_far = remote(cotf.at[t], cotf.at[t], ts.at[1], tr.at[1], tp=far)
    cot_sib.start()
    cot_far.start()
    send_all(0, xs, xr)
    zwait(0)
    zstart(1)

    loads[4].wait()

    def turn_filter(c):
        at = lanes(c)
        for p in range(2):
            rows_out(fv[p, :, at], fs, p, c)

    loop(8, turn_filter)
    zwait(1)
    zstart(2)
    send_all(1, fs, fr)
    zwait(2)
    zstart(3)
    remote(cotf.at[far], cotf.at[far], ts.at[1], tr.at[1], tp=far).wait_recv()
    cot_fwd = remote(cotf.at[far], cotf.at[far], ts.at[2], tr.at[2], tp=sib)
    cot_fwd.start()
    zwait(3)
    wstart(0, 1, 2, 3, 4, 5)

    wait_all(0, xs, xr)
    forward(xr, spec)
    wwait(0)
    wstart(6, 7)
    wwait(1, 2)
    wstart(8, 9, 10, 11)
    wait_all(1, fs, fr)
    inverse(spec, False, cs)
    send_all(2, cs, cr)
    wwait(4, 5)
    wstart(13, 14)
    wwait(8, 9)
    wstart(12)
    wwait(6, 7)
    wstart(15, 16)

    remote(cotf.at[sib], cotf.at[sib], ts.at[0], tr.at[0], tp=sib).wait_recv()
    fars = (1 - h) * 2 + (1 - core)
    remote(cotf.at[fars], cotf.at[fars], ts.at[2], tr.at[2], tp=sib).wait_recv()

    def grad_block(blk, first):
        left = cotf[blk]

        def one(n):
            at = pl.ds(pl.multiple_of(n * 256, 256), 256)
            right = wall[2 * blk : 2 * blk + 2, :, :, at].reshape(CH, 256)
            y = jnp.dot(left, right, preferred_element_type=F32)
            if first:
                gg[:, at] = y
            else:
                gg[:, at] += y

        loop(4, one)

    wwait(13, 14, 15, 16)
    grad_block(0, True)
    grad_block(1, False)
    wwait(3, 10, 11, 12)
    grad_block(2, False)
    grad_block(3, False)
    loads[5].wait()

    def turn_grad(c):
        at = lanes(c)
        rows_out(gg[:, at] * qv[:, at].astype(F32), gcs, None, c)

    loop(8, turn_grad)
    send_all(3, gcs, gcr)

    wait_all(2, cs, cr)

    def gate(c):
        at = lanes(c)
        y = back_at(cr, c).astype(BF)
        yf = y.astype(F32)
        stage[0, :, at] = (gg[:, at] * yf).astype(BF)
        conv[:, at] = (qv[:, at].astype(F32) * yf).astype(BF)

    loop(8, gate)
    gq_out = pltpu.make_async_copy(stage.at[0], gq, osem.at[0])
    gq_out.start()

    def out_block(blk):
        def one(n):
            right = wall[2 * blk + n // 2, pl.ds(lax.rem(n, 2) * 4, 4)].reshape(256, CH)
            at = pl.ds(pl.multiple_of(n * 256, 256), 256)
            part[blk, :, at] = lax.dot_general(
                conv[...], right, (((1,), (1,)), ((), ())), preferred_element_type=F32
            ).astype(BF)

        loop(4, one)

    psend = []
    for k, hh in ((0, 1 - h), (1, h)):
        out_block(hh * 2 + (1 - core))
        copy = remote(part.at[hh * 2 + (1 - core)], prec.at[hh], ts.at[3 + k], tr.at[3 + k], tp=sib)
        copy.start()
        psend.append(copy)
    out_block((1 - h) * 2 + core)
    out_block(h * 2 + core)
    remote(part.at[sib], prec.at[1 - h], ts.at[3], tr.at[3], tp=sib).wait_recv()
    osum[...] = (part[(1 - h) * 2 + core].astype(F32) + prec[1 - h].astype(F32)).astype(BF)
    osend = remote(osum, orec, ts.at[5], tr.at[5], tp=far)
    osend.start()

    wait_all(3, gcs, gcr)
    forward(gcr, gspec)

    def grad_filter(m):
        at = pl.ds(128 * m, 128)
        xre, xim = spec[at, 0:TOK].astype(F32), spec[at, TOK:].astype(F32)
        gre, gim = gspec[at, 0:TOK].astype(F32), gspec[at, TOK:].astype(F32)
        scale = 1.0 / LENGTH
        gfs[pl.ds(8 * m, 8), 0] = ((xre * gre + xim * gim) * scale).astype(BF).reshape(8, OWN, TOK)
        gfs[pl.ds(8 * m, 8), 1] = ((xre * gim - xim * gre) * scale).astype(BF).reshape(8, OWN, TOK)

    loop(8, grad_filter)
    send_all(4, gfs, gfr)
    inverse(gspec, True, gms)
    send_all(5, gms, gmr)

    remote(part.at[fars], prec.at[h], ts.at[4], tr.at[4], tp=sib).wait_recv()
    osend.wait_recv()
    stage[1] = (part[t].astype(F32) + prec[h].astype(F32) + orec[...].astype(F32)).astype(BF)
    out_out = pltpu.make_async_copy(stage.at[1], out, osem.at[1])
    out_out.start()

    wait_all(4, gfs, gfr)

    def filter_back(c):
        at = lanes(c)
        for p in range(2):
            fv[p, :, at] = gfr[pl.ds(8 * c, 8), p].reshape(128, TOK).astype(F32).T

    loop(8, filter_back)
    gf_out = pltpu.make_async_copy(fv, gf, osem.at[2])
    gf_out.start()
    wait_all(5, gms, gmr)

    def finish(c):
        at = lanes(c)
        y = back_at(gmr, c)
        stage[2, :, at] = (y * vv[:, at].astype(F32)).astype(BF)
        stage[3, :, at] = (y * kv[:, at].astype(F32)).astype(BF)

    loop(8, finish)
    gk_out = pltpu.make_async_copy(stage.at[2], gk, osem.at[3])
    gv_out = pltpu.make_async_copy(stage.at[3], gv, osem.at[4])
    gk_out.start()
    gv_out.start()

    for i, src, dst in ((0, xs, xr), (1, fs, fr), (2, cs, cr), (3, gcs, gcr), (4, gfs, gfr), (5, gms, gmr)):
        remote(src.at[pl.ds(0, NS - 1)], dst.at[pl.ds(0, NS - 1)], a2s.at[i], a2r.at[i], seq=s).wait_send()
    for k in range(4):
        zcopy(k, 1).wait_send()
        zcopy(k, -1).wait_send()
    for i in plan:
        wcopy(i).wait_send()
    for copy in (cot_sib, cot_far, cot_fwd, *psend, osend):
        copy.wait_send()
    for copy in (gq_out, out_out, gf_out, gk_out, gv_out):
        copy.wait()


def shards(queries, keys, values, filter_spectrum, weight, cotangent):
    wt = weight.T
    filt = filter_spectrum.reshape(2, TOK, CH)
    anywhere = pl.BlockSpec(memory_space=pl.ANY)
    vmem = pl.BlockSpec(memory_space=pltpu.VMEM)
    flat = jax.ShapeDtypeStruct((TOK, CH), BF)
    blocks = pltpu.VMEM((NS, OWN, TOK), BF)
    pairs = pltpu.VMEM((NS, 2, OWN, TOK), BF)
    whole = pltpu.VMEM((TOK, CH), BF)
    dma = pltpu.SemaphoreType.DMA
    out, gq, gk, gv, gf = pl.pallas_call(
        kernel,
        out_shape=(flat, flat, flat, flat, jax.ShapeDtypeStruct((2, TOK, CH), F32)),
        in_specs=[anywhere] * 6 + [vmem] * 6,
        out_specs=(anywhere,) * 5,
        scratch_shapes=[
            whole, whole, whole,
            pltpu.VMEM((4, TOK, CH), BF),
            pltpu.VMEM((2, TOK, CH), F32),
            pltpu.VMEM((NZ, NR, FEAT, CH), BF),
            blocks, blocks, pairs, pairs,
            pltpu.VMEM((ROWS, 2 * TOK), BF),
            pltpu.VMEM((ROWS, 2 * TOK), BF),
            pltpu.VMEM((2, ROWS, 128), F32),
            pltpu.VMEM((4, ROWS, 128), F32),
            blocks, blocks, blocks, blocks,
            pairs, pairs, blocks, blocks,
            whole,
            pltpu.VMEM((TOK, CH), F32),
            pltpu.VMEM((4, TOK, CH), BF),
            pltpu.VMEM((2, TOK, CH), BF),
            whole, whole,
            pltpu.VMEM((4, TOK, CH), BF),
            dma((6,)), dma((5,)), dma((6,)), dma((6,)),
            dma((2, 4)), dma((2, 4)), dma((17,)), dma((17,)), dma((6,)), dma((6,)),
        ],
        compiler_params=pltpu.CompilerParams(
            collective_id=0, has_side_effects=True, vmem_limit_bytes=56 * 1024 * 1024
        ),
    )(keys, values, queries, cotangent, filt, wt, *tables())
    return out, gq, gk, gv, gf.reshape(2, 1, TOK, CH)


def solution(mesh):
    io = P("seq", "tp")
    spectrum = P(None, "seq", None, "tp")
    return jax.shard_map(
        shards,
        mesh=mesh,
        in_specs=(io, io, io, spectrum, P("tp", "seq"), io),
        out_specs=(io, io, io, io, spectrum),
        check_vma=False,
    )
```

time: 605 us -> 190 us (0.31)
  waiting for transfers between devices: 401 us -> 0 us
  Pallas kernels: 0 us -> 181 us
  starting transfers between devices: 54.8 us -> 0 us
  blocking collectives: 46.9 us -> 0 us
  local copies, waits for them, and re-layouts: 38.4 us -> 6.8 us
  other arithmetic: 22.1 us -> 0 us
  matrix products: 21.6 us -> 0 us
  between operations: 14.3 us -> 0.67 us
    all_gather x2 -> x0, waiting for transfers between devices: 331 us -> none  [the longest x1 310 us: shards(): full_weight = lax.all_gather(weight, 'seq', axis=1, tiled=True)]
    pallas_call x0 -> x1, Pallas kernels: none -> 181 us  [shards(): pl.pallas_call(kernel, out_shape=(flat, flat, flat, flat, jax.ShapeDtypeS...]
    all_to_all x6 -> x0, waiting for transfers between devices: 69.2 us -> none  [the longest x2 26.5 us: forward_spectrum(): lax.all_to_all(turned, 'seq', split_axis=1, concat_axis=2, tiled=True)]
    all_to_all x6 -> x0, starting transfers between devices: 54.4 us -> none  [the longest x2 27.8 us: forward_spectrum(): lax.all_to_all(signal.reshape(tok_rows, 1, channels), 'seq', split_axis=0...]
    all_to_all x2 -> x0, blocking collectives: 46.9 us -> none  [the longest x1 25.9 us: inverse_signal(): lax.all_to_all(turned, 'seq', split_axis=2, concat_axis=1, tiled=True)]
    dot_general x10 -> x0, matrix products: 21.6 us -> none  [the longest x1 7.67 us: shards(): jnp.dot(gated, full_weight, preferred_element_type=jnp.float32)]
    another operation x6 -> x0, local copies, waits for them, and re-layouts: 13 us -> none  [the longest x4 6.88 us: rotate(): jnp.stack([real_part * cosine - imag_part * sine_part, imag_part * cosine...]
    all_to_all x2 -> x0, other arithmetic: 6.9 us -> none  [forward_spectrum(): lax.all_to_all(signal.reshape(tok_rows, 1, channels), 'seq', split_axis=0...]
  transfers between devices with their start and end apart: 9 -> 0, of which waited for: 7 -> 0; matrix products, arithmetic and copies ran while one was open for 7% -> 0% of each run, Pallas kernels for 0% -> 0%
where the time goes in v1:
time: 190 us; the launch traced here: 188 us
  Pallas kernels  181 us (95%)
  local copies, waits for them, and re-layouts  6.8 us (4%)
    pallas_call x1, Pallas kernels, shards(): pl.pallas_call(kernel, out_shape=(flat, flat, flat, flat, jax.ShapeDtypeS...  181 us
    unnamed x11, local copies, waits for them, and re-layouts  6.8 us

profile of v1, /device:TPU:8, one launch (start us, length us, event | category | flops | bytes accessed | tf_op | source)
XLA Modules:
  0.0 188.3 jit_solution(9889587594473832775)
XLA Ops:
  0.6 180.8 %shard_map.155 = (bf16[256,1024]{1,0:T(8,128)(2,1)}, bf16[256,1024]{1,0:T(8,128)(2,1)}, bf16[256,1024]{1,0:T(8,128)(2,1)}, bf16[256,1024]{1,0:T(8,128)(2,1)}, f32[2,256,1024]{2,1,0:T(8,128)}) custom-call(bf16[256,1024]{1,0:T(8,128)(2,1)} %keys.1, bf16[256,1024]{1,0:T(8,128)(2,1)} %values.1, bf16[256,1024]{1,0:T(8,128)(2,1)} %queries.1, ...), custom_call_target="tpu_custom_call" | custom-call | tf_op jit(solution)/shard_map/pallas_call | solution.py:436
  181.5 0.0 copy-start.2
  181.5 0.0 copy-start.1
  181.5 0.0 copy-start
  181.5 2.0 %copy.23 = bf16[256,1024]{1,0:T(8,128)(2,1)} copy(bf16[256,1024]{1,0:T(8,128)(2,1)} %get-tuple-element.25) | data formatting | bytes 1048576
  183.5 1.9 copy.24
  185.4 0.0 copy-done.2
  185.4 0.8 copy.25
  186.2 0.0 copy-done.1
  186.2 0.8 copy.26
  187.0 0.0 copy-done
  187.0 1.3 copy.27
Async XLA Ops:
  181.5 3.9 %copy-start.2 = (bf16[256,1024]{1,0:T(8,128)(2,1)S(1)}, bf16[256,1024]{1,0:T(8,128)(2,1)}, u32[]{:S(2)}) copy-start(bf16[256,1024]{1,0:T(8,128)(2,1)} %get-tuple-element.27) | copy-start | bytes 1572868
  181.5 4.7 %copy-start.1 = (bf16[256,1024]{1,0:T(8,128)(2,1)S(1)}, bf16[256,1024]{1,0:T(8,128)(2,1)}, u32[]{:S(2)}) copy-start(bf16[256,1024]{1,0:T(8,128)(2,1)} %get-tuple-element.28) | copy-start | bytes 1572868
  181.5 5.5 %copy-start = (f32[2,256,1024]{2,1,0:T(8,128)S(1)}, f32[2,256,1024]{2,1,0:T(8,128)}, u32[]{:S(2)}) copy-start(f32[2,256,1024]{2,1,0:T(8,128)} %get-tuple-element.14) | copy-start | bytes 6291460

commit v2 on v1

v2 whole, which is shorter than its diff:
```python
import math

import jax
import jax.numpy as jnp
import numpy as np
from jax import lax
from jax.experimental import pallas as pl
from jax.experimental.pallas import tpu as pltpu
from jax.sharding import PartitionSpec as P

MESH = pl.DeviceIdType.MESH
BF = jnp.bfloat16
F32 = jnp.float32

NZ, NY, NX = 8, 2, 4
NS = NZ * NY * NX
NR = NY * NX
TOK = 256
CH = 1024
OWN = CH // NS
FEAT = 64
LENGTH = TOK * NS
ROWS = NS * OWN


def tables():
    b = np.arange(NS)
    ang = 2.0 * np.pi / NS * (b[:, None] * b[None, :] % NS)
    wb = np.concatenate([np.cos(ang), -np.sin(ang)], 0)
    wbi = np.concatenate([np.cos(ang), -np.sin(ang)], 1)
    a = np.arange(TOK)
    ang = 2.0 * np.pi / TOK * (a[:, None] * a[None, :] % TOK)
    c, s = np.cos(ang), np.sin(ang)
    fwd = np.block([[c, -s], [s, c]])
    inv = np.block([[c, s], [-s, c]])
    ang = 2.0 * np.pi / LENGTH * (b[:, None] * a[None, :] % LENGTH)
    low = [jnp.asarray(t.astype(np.float32)).astype(BF) for t in (wb, wbi, fwd, inv)]
    return (*low, jnp.asarray(np.cos(ang).astype(np.float32)), jnp.asarray(np.sin(ang).astype(np.float32)))


def kernel(
    keys, values, queries, cot, filt, wt, wb, wbi, dfa, dia, cosr, sinr,
    out, gq, gfr, gmr,
    kv, vv, qv, cotg, cots, fv, wall, xs, xr, fs, fr, spec, gspec, s32, t32, cs, cr, gcs, gcr, gfs, gms,
    gat, gg, gsend, grecv, part, prec, ssum, orec, stage,
    lsem, osem, a2s, a2r, a2l, zs, zr, ws, wr, wfs, wfr, ts, tr, gs, gr, ps, pr,
):
    s = lax.axis_index("seq")
    t = lax.axis_index("tp")
    z, r = s // NR, lax.rem(s, NR)
    yl, x = r // NX, lax.rem(r, NX)
    h, core = t // 2, lax.rem(t, 2)
    sib = h * 2 + (1 - core)
    far = (1 - h) * 2 + core
    fars = (1 - h) * 2 + (1 - core)
    beside = z * NR + (1 - yl) * NX + x

    def load(i, src, dst):
        return pltpu.make_async_copy(src, dst, lsem.at[i])

    def columns(half, zz):
        return pl.ds(pl.multiple_of(512 * zz + 256 * half, 256), 256)

    loads = [
        load(0, wt, wall.at[z, x]),
        load(1, keys, kv),
        load(2, values, vv),
        load(3, filt, fv),
        load(4, queries, qv),
    ]
    for zz in range(2):
        at = pl.ds(256 * zz, 256)
        loads.append(load(5 + zz, cot.at[:, columns(yl, zz)], cotg.at[0, t, :, at]))
        loads.append(load(7 + zz, cot.at[:, columns(1 - yl, zz)], cots.at[:, at]))
    for one in loads:
        one.start()

    barrier = pltpu.get_barrier_semaphore()

    def greet(i, carry):
        pl.semaphore_signal(barrier, inc=1, device_id={"seq": lax.rem(s + i, NS)}, device_id_type=MESH)
        return carry

    lax.fori_loop(1, NS, greet, 0)
    for i in range(1, 4):
        pl.semaphore_signal(barrier, inc=1, device_id={"tp": lax.rem(t + i, 4)}, device_id_type=MESH)
    pl.semaphore_signal(barrier, inc=1, device_id={"seq": beside, "tp": far}, device_id_type=MESH)

    def rows_out(val, dst, at, c):
        moved = val.T.astype(BF).reshape(8, OWN, TOK)
        if at is None:
            dst[pl.ds(8 * c, 8)] = moved
        else:
            dst[pl.ds(8 * c, 8), at] = moved

    def lanes(c):
        return pl.ds(pl.multiple_of(c * 128, 128), 128)

    def loop(n, body):
        def step(i, carry):
            body(i)
            return carry

        lax.fori_loop(0, n, step, 0)

    loads[1].wait()
    loads[2].wait()

    def mix(c):
        at = lanes(c)
        rows_out(kv[:, at].astype(F32) * vv[:, at].astype(F32), xs, None, c)

    loop(8, mix)
    for i in (0, 5, 6, 7, 8):
        loads[i].wait()

    pl.semaphore_wait(barrier, NS - 1 + 3 + 1)

    def remote(src, dst, ss, rs, **to):
        return pltpu.make_async_remote_copy(
            src_ref=src, dst_ref=dst, send_sem=ss, recv_sem=rs, device_id=to, device_id_type=MESH
        )

    def send_all(i, src, dst):
        def one(k, carry):
            d = lax.rem(s + k, NS)
            remote(src.at[d], dst.at[s], a2s.at[i], a2r.at[i], seq=d).start()
            return carry

        pltpu.make_async_copy(src.at[s], dst.at[s], a2l.at[i]).start()
        lax.fori_loop(1, NS, one, 0)

    def wait_all(i, src, dst):
        remote(src.at[pl.ds(0, NS - 1)], dst.at[pl.ds(0, NS - 1)], a2s.at[i], a2r.at[i], seq=s).wait_recv()
        pltpu.make_async_copy(src.at[s], dst.at[s], a2l.at[i]).wait()

    def zdev(k):
        return lax.rem(z + k + NZ, NZ)

    def zcopy(k, way):
        src = wall.at[zdev(-k * way), x]
        if k == 3:
            src = wall.at[zdev(-k * way), x, pl.ds(0 if way > 0 else FEAT // 2, FEAT // 2)]
        i = 0 if way > 0 else 1
        return remote(src, src, zs.at[i, k], zr.at[i, k], seq=zdev(way) * NR + r)

    def zwait(k):
        for i, way in ((0, 1), (1, -1)):
            src = wall.at[zdev(-(k + 1) * way), x]
            if k == 3:
                src = wall.at[zdev(-(k + 1) * way), x, pl.ds(0 if way > 0 else FEAT // 2, FEAT // 2)]
            remote(src, src, zs.at[i, k], zr.at[i, k], seq=zdev(way) * NR + r).wait_recv()

    def zstart(k):
        zcopy(k, 1).start()
        zcopy(k, -1).start()

    batches = ((0,), (-1, 1), (-2, 2), (-3, 3), (4,))

    def xdev(k):
        return lax.rem(x + k + NX, NX)

    def xcopy(off, way, back=False):
        i, j = off + 3, 0 if way > 0 else 1
        ref = wall.at[zdev(off), xdev(-way if back else 0)]
        return remote(ref, ref, ws.at[i, j], wr.at[i, j], seq=z * NR + yl * NX + xdev(way))

    def xfwd(off, way, back=False):
        i, j = off + 3, 0 if way > 0 else 1
        half = pl.ds(0 if way > 0 else FEAT // 2, FEAT // 2)
        ref = wall.at[zdev(off), xdev(-2 * way if back else -way), half]
        return remote(ref, ref, wfs.at[i, j], wfr.at[i, j], seq=z * NR + yl * NX + xdev(way))

    def xstart(k):
        for off in batches[k]:
            xcopy(off, 1).start()
            xcopy(off, -1).start()

    def xpass(k):
        for off in batches[k]:
            for way in (1, -1):
                xcopy(off, way, True).wait_recv()
                xfwd(off, way).start()

    def xwait(k):
        for off in batches[k]:
            for way in (1, -1):
                xfwd(off, way, True).wait_recv()

    def forward(src, dst):
        def widen(m):
            wide = src[pl.ds(8 * m, 8)].reshape(128, TOK).astype(F32)
            for lane in range(2):
                s32[lane, pl.ds(128 * m, 128)] = wide[:, 128 * lane : 128 * lane + 128]

        loop(8, widen)
        for c in range(OWN):
            at = pl.ds(c, NS, stride=OWN)
            taken = jnp.concatenate([s32[lane, at, :] for lane in range(2)], 1).astype(BF)
            y = jnp.dot(wb[...], taken, preferred_element_type=F32)
            re, im = y[:NS], y[NS:]
            tre = re * cosr[...] + im * sinr[...]
            tim = im * cosr[...] - re * sinr[...]
            for lane in range(2):
                t32[lane, at, :] = tre[:, 128 * lane : 128 * lane + 128]
                t32[2 + lane, at, :] = tim[:, 128 * lane : 128 * lane + 128]

        def second(m):
            at = pl.ds(128 * m, 128)
            left = jnp.concatenate([t32[lane, at] for lane in range(4)], 1).astype(BF)
            dst[at] = jnp.dot(left, dfa[...], preferred_element_type=F32).astype(BF)

        loop(8, second)

    def filter_at(m):
        at = pl.ds(8 * m, 8)
        return fr[at, 0].reshape(128, TOK).astype(F32), fr[at, 1].reshape(128, TOK).astype(F32)

    def inverse(src, conj, dst):
        def first(m):
            at = pl.ds(128 * m, 128)
            sre, sim = src[at, 0:TOK].astype(F32), src[at, TOK:].astype(F32)
            fre, fim = filter_at(m)
            if conj:
                fim = -fim
            y = jnp.concatenate([sre * fre - sim * fim, sre * fim + sim * fre], 1).astype(BF)
            o = jnp.dot(y, dia[...], preferred_element_type=F32)
            for lane in range(4):
                t32[lane, at] = o[:, 128 * lane : 128 * lane + 128]

        loop(8, first)
        for c in range(OWN):
            at = pl.ds(c, NS, stride=OWN)
            re = jnp.concatenate([t32[lane, at, :] for lane in range(2)], 1)
            im = jnp.concatenate([t32[2 + lane, at, :] for lane in range(2)], 1)
            tre = re * cosr[...] - im * sinr[...]
            tim = im * cosr[...] + re * sinr[...]
            both = jnp.concatenate([tre, tim], 0).astype(BF)
            o = jnp.dot(wbi[...], both, preferred_element_type=F32) * (1.0 / LENGTH)
            for lane in range(2):
                s32[lane, at, :] = o[:, 128 * lane : 128 * lane + 128]

        def narrow(m):
            wide = jnp.concatenate([s32[lane, pl.ds(128 * m, 128)] for lane in range(2)], 1)
            dst[pl.ds(8 * m, 8)] = wide.astype(BF).reshape(8, OWN, TOK)

        loop(8, narrow)

    def back_at(src, c):
        return src[pl.ds(8 * c, 8)].reshape(128, TOK).astype(F32).T

    zstart(0)
    xstart(0)
    half_sib = remote(cotg.at[0, t], cotg.at[0, t], ts.at[0], tr.at[0], tp=sib)
    half_far = remote(cotg.at[0, t], cotg.at[0, t], ts.at[1], tr.at[1], tp=far)
    half_beside = remote(cots, cotg.at[1, t], ts.at[2], tr.at[2], seq=beside)
    half_across = remote(cots, cotg.at[1, t], ts.at[3], tr.at[3], seq=beside, tp=far)
    send_all(0, xs, xr)
    for copy in (half_sib, half_far, half_beside, half_across):
        copy.start()
    zwait(0)
    zstart(1)
    xstart(1)
    loads[3].wait()

    def turn_filter(c):
        at = lanes(c)
        for p in range(2):
            rows_out(fv[p, :, at], fs, p, c)

    loop(4, turn_filter)
    zwait(1)
    zstart(2)
    xstart(2)
    xpass(0)
    loop(4, lambda c: turn_filter(c + 4))
    zwait(2)
    zstart(3)
    xstart(3)
    xpass(1)
    zwait(3)
    xstart(4)
    send_all(1, fs, fr)
    xpass(2)
    arrived = []
    for i, (tok, blk) in enumerate(((0, far), (1, t), (1, far))):
        ref = cotg.at[tok, blk]
        remote(ref, ref, ts.at[1 + i], tr.at[1 + i], tp=sib).wait_recv()
        on = remote(ref, ref, ts.at[4 + i], tr.at[4 + i], tp=sib)
        on.start()
        arrived.append(on)
    xpass(3)

    wait_all(0, xs, xr)
    forward(xr, spec)
    xpass(4)
    for i, (tok, blk) in ((0, (0, sib)), (4, (0, fars)), (5, (1, sib)), (6, (1, fars))):
        ref = cotg.at[tok, blk]
        remote(ref, ref, ts.at[i], tr.at[i], tp=sib).wait_recv()
    wait_all(1, fs, fr)
    inverse(spec, False, cs)
    send_all(2, cs, cr)
    for k in range(5):
        xwait(k)

    def quarter(n):
        return pl.ds(256 * n, 256)

    def grad_half(tok, n):
        total = None
        for blk in range(4):
            right = wall[2 * blk : 2 * blk + 2, :, :, quarter(n)].reshape(512, 256)
            y = jnp.dot(cotg[tok, blk], right, preferred_element_type=F32)
            total = y if total is None else total + y
        return total

    def grad_copy(n):
        return remote(gsend.at[:, quarter(n)], grecv.at[:, quarter(n)], gs.at[n], gr.at[n], seq=beside)

    for n in range(4):
        gsend[:, quarter(n)] = grad_half(1, n).astype(BF)
        grad_copy(n).start()
    for n in range(4):
        gg[:, quarter(n)] = grad_half(0, n)
    loads[4].wait()

    def turn_grad(c):
        at = lanes(c)
        y = gg[:, at] + grecv[:, at].astype(F32)
        gg[:, at] = y
        rows_out(y * qv[:, at].astype(F32), gcs, None, c)

    for n in range(4):
        grad_copy(n).wait_recv()
        turn_grad(2 * n)
        turn_grad(2 * n + 1)
    send_all(3, gcs, gcr)

    wait_all(2, cs, cr)

    def gate(c):
        at = lanes(c)
        y = back_at(cr, c).astype(BF)
        yf = y.astype(F32)
        stage[0, :, at] = (gg[:, at] * yf).astype(BF)
        gat[0, :, at] = (qv[:, at].astype(F32) * yf).astype(BF)

    loop(8, gate)
    gat_copy = remote(gat.at[0], gat.at[1], ts.at[7], tr.at[7], seq=beside)
    gat_copy.start()
    gq_out = pltpu.make_async_copy(stage.at[0], gq, osem.at[0])
    gq_out.start()

    def out_blocks(tok):
        def one(blk):
            for zz in range(2):
                right = wall[2 * blk + zz].reshape(256, CH)
                part[tok, blk, :, pl.ds(256 * zz, 256)] = lax.dot_general(
                    gat[tok], right, (((1,), (1,)), ((), ())), preferred_element_type=F32
                ).astype(BF)

        loop(4, one)

    out_blocks(0)

    wait_all(3, gcs, gcr)
    forward(gcr, gspec)

    def grad_filter(m):
        at = pl.ds(128 * m, 128)
        xre, xim = spec[at, 0:TOK].astype(F32), spec[at, TOK:].astype(F32)
        gre, gim = gspec[at, 0:TOK].astype(F32), gspec[at, TOK:].astype(F32)
        scale = 1.0 / LENGTH
        gfs[pl.ds(8 * m, 8), 0] = ((xre * gre + xim * gim) * scale).astype(BF).reshape(8, OWN, TOK)
        gfs[pl.ds(8 * m, 8), 1] = ((xre * gim - xim * gre) * scale).astype(BF).reshape(8, OWN, TOK)

    loop(8, grad_filter)
    send_all(4, gfs, gfr)
    inverse(gspec, True, gms)
    send_all(5, gms, gmr)

    gat_copy.wait_recv()
    out_blocks(1)

    def core_copy(tok, hh):
        i = 2 * tok + hh
        return remote(part.at[tok, hh * 2 + (1 - core)], prec.at[tok, hh], ps.at[i], pr.at[i], tp=sib)

    pairs = ((0, 0), (0, 1), (1, 0), (1, 1))
    for tok, hh in pairs:
        core_copy(tok, hh).start()
    for tok, hh in pairs:
        core_copy(tok, hh).wait_recv()
        ssum[tok, hh] = (part[tok, hh * 2 + core].astype(F32) + prec[tok, hh].astype(F32)).astype(BF)
    sum_far = remote(ssum.at[0, 1 - h], orec.at[0], ts.at[8], tr.at[8], tp=far)
    sum_beside = remote(ssum.at[1, h], orec.at[1], ts.at[9], tr.at[9], seq=beside)
    sum_across = remote(ssum.at[1, 1 - h], orec.at[2], ts.at[10], tr.at[10], seq=beside, tp=far)
    sums = (sum_far, sum_beside, sum_across)
    for copy in sums:
        copy.start()
    for copy in sums:
        copy.wait_recv()
    for zz in range(2):
        at = pl.ds(256 * zz, 256)
        mine = ssum[0, h, :, at].astype(F32) + orec[0, :, at].astype(F32)
        stage[1, :, columns(yl, zz)] = mine.astype(BF)
        other = orec[1, :, at].astype(F32) + orec[2, :, at].astype(F32)
        stage[1, :, columns(1 - yl, zz)] = other.astype(BF)
    out_out = pltpu.make_async_copy(stage.at[1], out, osem.at[1])
    out_out.start()

    wait_all(4, gfs, gfr)
    wait_all(5, gms, gmr)

    for i, src, dst in ((0, xs, xr), (1, fs, fr), (2, cs, cr), (3, gcs, gcr), (4, gfs, gfr), (5, gms, gmr)):
        remote(src.at[pl.ds(0, NS - 1)], dst.at[pl.ds(0, NS - 1)], a2s.at[i], a2r.at[i], seq=s).wait_send()
    for k in range(4):
        zcopy(k, 1).wait_send()
        zcopy(k, -1).wait_send()
    for batch in batches:
        for off in batch:
            for way in (1, -1):
                xcopy(off, way).wait_send()
                xfwd(off, way).wait_send()
    for copy in (half_sib, half_far, half_beside, half_across, *arrived, gat_copy, *sums):
        copy.wait_send()
    for n in range(4):
        grad_copy(n).wait_send()
    for tok, hh in pairs:
        core_copy(tok, hh).wait_send()
    gq_out.wait()
    out_out.wait()


def finish(out_in, gq_in, gfr, gmr, keys, values, out, gq, gk, gv, gf):
    out[...] = out_in[...]
    gq[...] = gq_in[...]
    for p in range(2):
        gf[p] = gfr[:, p].reshape(128, TOK).astype(F32).T
    y = gmr[...].reshape(128, TOK).astype(F32).T
    gk[...] = (y * values[...].astype(F32)).astype(BF)
    gv[...] = (y * keys[...].astype(F32)).astype(BF)


def shards(queries, keys, values, filter_spectrum, weight, cotangent):
    wt = weight.T
    filt = filter_spectrum.reshape(2, TOK, CH)
    anywhere = pl.BlockSpec(memory_space=pl.ANY)
    vmem = pl.BlockSpec(memory_space=pltpu.VMEM)
    flat = jax.ShapeDtypeStruct((TOK, CH), BF)
    blocks = pltpu.VMEM((NS, OWN, TOK), BF)
    pairs = pltpu.VMEM((NS, 2, OWN, TOK), BF)
    whole = pltpu.VMEM((TOK, CH), BF)
    dma = pltpu.SemaphoreType.DMA
    blocks_out = jax.ShapeDtypeStruct((NS, OWN, TOK), BF)
    pairs_out = jax.ShapeDtypeStruct((NS, 2, OWN, TOK), BF)
    out, gq, gfr, gmr = pl.pallas_call(
        kernel,
        out_shape=(flat, flat, pairs_out, blocks_out),
        in_specs=[anywhere] * 6 + [vmem] * 6,
        out_specs=(anywhere,) * 4,
        scratch_shapes=[
            whole, whole, whole,
            pltpu.VMEM((2, 4, TOK, 512), BF),
            pltpu.VMEM((TOK, 512), BF),
            pltpu.VMEM((2, TOK, CH), F32),
            pltpu.VMEM((NZ, NX, FEAT, CH), BF),
            blocks, blocks, pairs, pairs,
            pltpu.VMEM((ROWS, 2 * TOK), BF),
            pltpu.VMEM((ROWS, 2 * TOK), BF),
            pltpu.VMEM((2, ROWS, 128), F32),
            pltpu.VMEM((4, ROWS, 128), F32),
            blocks, blocks, blocks, blocks,
            pairs, blocks,
            pltpu.VMEM((2, TOK, CH), BF),
            pltpu.VMEM((TOK, CH), F32),
            whole, whole,
            pltpu.VMEM((2, 4, TOK, 512), BF),
            pltpu.VMEM((2, 2, TOK, 512), BF),
            pltpu.VMEM((2, 2, TOK, 512), BF),
            pltpu.VMEM((3, TOK, 512), BF),
            pltpu.VMEM((2, TOK, CH), BF),
            dma((9,)), dma((2,)), dma((6,)), dma((6,)), dma((6,)),
            dma((2, 4)), dma((2, 4)), dma((8, 2)), dma((8, 2)), dma((8, 2)), dma((8, 2)),
            dma((11,)), dma((11,)), dma((4,)), dma((4,)), dma((4,)), dma((4,)),
        ],
        compiler_params=pltpu.CompilerParams(
            collective_id=0, has_side_effects=True, vmem_limit_bytes=56 * 1024 * 1024
        ),
    )(keys, values, queries, cotangent, filt, wt, *tables())
    lane = pl.BlockSpec((TOK, 128), lambda c: (0, c))
    out, gq, gk, gv, gf = pl.pallas_call(
        finish,
        grid=(8,),
        out_shape=(flat, flat, flat, flat, jax.ShapeDtypeStruct((2, TOK, CH), F32)),
        in_specs=[
            lane,
            lane,
            pl.BlockSpec((8, 2, OWN, TOK), lambda c: (c, 0, 0, 0)),
            pl.BlockSpec((8, OWN, TOK), lambda c: (c, 0, 0)),
            lane,
            lane,
        ],
        out_specs=(lane, lane, lane, lane, pl.BlockSpec((2, TOK, 128), lambda c: (0, 0, c))),
        compiler_params=pltpu.CompilerParams(vmem_limit_bytes=56 * 1024 * 1024),
    )(out, gq, gfr, gmr, keys, values)
    return out, gq, gk, gv, gf.reshape(2, 1, TOK, CH)


def solution(mesh):
    io = P("seq", "tp")
    spectrum = P(None, "seq", None, "tp")
    return jax.shard_map(
        shards,
        mesh=mesh,
        in_specs=(io, io, io, spectrum, P("tp", "seq"), io),
        out_specs=(io, io, io, io, spectrum),
        check_vma=False,
    )
```

time: 190 us -> 152 us (0.80)
  Pallas kernels: 181 us -> 151 us
  local copies, waits for them, and re-layouts: 6.8 us -> 0 us
    pallas_call x1 -> x2, Pallas kernels: 181 us -> 151 us  [the longest x1 144 us: shards(): pl.pallas_call(kernel, out_shape=(flat, flat, pairs_out, blocks_out), in_...]
    unnamed x11 -> x0, local copies, waits for them, and re-layouts: 6.8 us -> none
where the time goes in v2:
time: 152 us
  Pallas kernels  151 us (99%)
    pallas_call x1, Pallas kernels, shards(): pl.pallas_call(kernel, out_shape=(flat, flat, pairs_out, blocks_out), in_...  144 us
    pallas_call x1, Pallas kernels, shards(): pl.pallas_call(finish, grid=(8,), out_shape=(flat, flat, flat, flat, jax....  6.68 us

profile of v2, /device:TPU:8, one launch (start us, length us, event | category | flops | bytes accessed | tf_op | source)
XLA Modules:
  0.0 151.8 jit_solution(970051985055853098)
XLA Ops:
  0.6 144.5 %shard_map.155 = (bf16[256,1024]{1,0:T(8,128)(2,1)}, bf16[256,1024]{1,0:T(8,128)(2,1)}, bf16[64,2,16,256]{3,2,1,0:T(8,128)(2,1)}, bf16[64,16,256]{2,1,0:T(8,128)(2,1)}) custom-call(bf16[256,1024]{1,0:T(8,128)(2,1)} %keys.3, bf16[256,1024]{1,0:T(8,128)(2,1)} %values.3, bf16[256,1024]{1,0:T(8,128)(2,1)} %queries.1, bf16[256,1024]{1,0:T(8,128)(2,1)} %cot.1, ...), custom_call_target="tpu_custom_call" | custom-call | tf_op jit(solution)/shard_map/pallas_call | solution.py:457
  145.1 6.7 %shard_map.156 = (bf16[256,1024]{1,0:T(8,128)(2,1)}, bf16[256,1024]{1,0:T(8,128)(2,1)}, bf16[256,1024]{1,0:T(8,128)(2,1)}, bf16[256,1024]{1,0:T(8,128)(2,1)}, f32[2,256,1024]{2,1,0:T(8,128)}) custom-call(bf16[256,1024]{1,0:T(8,128)(2,1)} %get-tuple-element.14.out_in, bf16[256,1024]{1,0:T(8,128)(2,1)} %get-tuple-element.15.gq_in, ...), custom_call_target="tpu_custom_call" | custom-call | tf_op jit(solution)/shard_map/pallas_call | solution.py:492

commit v3 on v2

--- a/solution.py
+++ b/solution.py
@@ -39,11 +39,11 @@
 
 
 def kernel(
-    keys, values, queries, cot, filt, wt, wb, wbi, dfa, dia, cosr, sinr,
+    keys, values, queries, cot, filt, wt, wb_in, wbi_in, dfa_in, dia_in, cos_in, sin_in,
     out, gq, gfr, gmr,
-    kv, vv, qv, cotg, cots, fv, wall, xs, xr, fs, fr, spec, gspec, s32, t32, cs, cr, gcs, gcr, gfs, gms,
+    wb, wbi, dfa, dia, cosr, sinr, kv, vv, qv, cotg, cots, fv, wall, xs, xr, fs, fr, spec, gspec, s32, t32, cs, cr, gcs, gcr, gfs, gms,
     gat, gg, gsend, grecv, part, prec, ssum, orec, stage,
-    lsem, osem, a2s, a2r, a2l, zs, zr, ws, wr, wfs, wfr, ts, tr, gs, gr, ps, pr,
+    row_sem, side_sem, lsem, osem, a2s, a2r, a2l, zs, zr, ws, wr, wfs, wfr, ts, tr, gs, gr, ps, pr,
 ):
     s = lax.axis_index("seq")
     t = lax.axis_index("tp")
@@ -72,16 +72,18 @@
         at = pl.ds(256 * zz, 256)
         loads.append(load(5 + zz, cot.at[:, columns(yl, zz)], cotg.at[0, t, :, at]))
         loads.append(load(7 + zz, cot.at[:, columns(1 - yl, zz)], cots.at[:, at]))
+    tables_in = ((wb_in, wb), (dfa_in, dfa), (cos_in, cosr), (sin_in, sinr), (dia_in, dia), (wbi_in, wbi))
+    for i, (src, dst) in enumerate(tables_in):
+        loads.append(load(9 + i, src, dst))
     for one in loads:
         one.start()
 
     barrier = pltpu.get_barrier_semaphore()
 
-    def greet(i, carry):
-        pl.semaphore_signal(barrier, inc=1, device_id={"seq": lax.rem(s + i, NS)}, device_id_type=MESH)
-        return carry
-
-    lax.fori_loop(1, NS, greet, 0)
+    line = [zz_ * NR + r for zz_ in (lax.rem(z + k, NZ) for k in range(1, NZ))]
+    row = [z * NR + yl * NX + lax.rem(x + k, NX) for k in range(1, NX)]
+    for d in (*line, *row, beside):
+        pl.semaphore_signal(barrier, inc=1, device_id={"seq": d}, device_id_type=MESH)
     for i in range(1, 4):
         pl.semaphore_signal(barrier, inc=1, device_id={"tp": lax.rem(t + i, 4)}, device_id_type=MESH)
     pl.semaphore_signal(barrier, inc=1, device_id={"seq": beside, "tp": far}, device_id_type=MESH)
@@ -103,32 +105,52 @@
 
         lax.fori_loop(0, n, step, 0)
 
-    loads[1].wait()
-    loads[2].wait()
-
     def mix(c):
         at = lanes(c)
         rows_out(kv[:, at].astype(F32) * vv[:, at].astype(F32), xs, None, c)
 
-    loop(8, mix)
-    for i in (0, 5, 6, 7, 8):
-        loads[i].wait()
-
-    pl.semaphore_wait(barrier, NS - 1 + 3 + 1)
+    loads[0].wait()
+    for one in loads[5:9]:
+        one.wait()
+
+    pl.semaphore_wait(barrier, len(line) + len(row) + 1 + 3 + 1)
 
     def remote(src, dst, ss, rs, **to):
         return pltpu.make_async_remote_copy(
             src_ref=src, dst_ref=dst, send_sem=ss, recv_sem=rs, device_id=to, device_id_type=MESH
         )
 
-    def send_all(i, src, dst):
-        def one(k, carry):
-            d = lax.rem(s + k, NS)
-            remote(src.at[d], dst.at[s], a2s.at[i], a2r.at[i], seq=d).start()
-            return carry
-
-        pltpu.make_async_copy(src.at[s], dst.at[s], a2l.at[i]).start()
-        lax.fori_loop(1, NS, one, 0)
+    def owner(block):
+        zz = lax.rem(block, 16) // 2
+        return zz * NR + lax.rem(block, 2) * NX + lax.rem(block // 16 + zz, NX)
+
+    own = lax.rem(x + NZ - z, NX) * 16 + z * 2 + yl
+
+    def send(i, src, dst, d):
+        @pl.when(d != s)
+        def _():
+            remote(src, dst, a2s.at[i], a2r.at[i], seq=d).start()
+
+        @pl.when(d == s)
+        def _():
+            pltpu.make_async_copy(src, dst, a2l.at[i]).start()
+
+    def send_owners(i, src, dst, first=0, count=NS):
+        def one(k):
+            block = first + lax.rem(own + k, count)
+            send(i, src.at[block], dst.at[s], owner(block))
+
+        loop(count, one)
+
+    def send_home(i, src, dst, m):
+        def one(k):
+            d = m * NR + lax.rem(r + k, NR)
+            send(i, src.at[d], dst.at[own], d)
+
+        loop(NR, one)
+
+    def ring_z(body):
+        loop(NZ, lambda k: body(lax.rem(z + k, NZ)))
 
     def wait_all(i, src, dst):
         remote(src.at[pl.ds(0, NS - 1)], dst.at[pl.ds(0, NS - 1)], a2s.at[i], a2r.at[i], seq=s).wait_recv()
@@ -187,11 +209,11 @@
             for way in (1, -1):
                 xfwd(off, way, True).wait_recv()
 
-    def forward(src, dst):
+    def forward(src, dst, then=None):
         def widen(m):
             wide = src[pl.ds(8 * m, 8)].reshape(128, TOK).astype(F32)
             for lane in range(2):
-                s32[lane, pl.ds(128 * m, 128)] = wide[:, 128 * lane : 128 * lane + 128]
+                s32[lane, pl.ds(pl.multiple_of(128 * m, 128), 128)] = wide[:, 128 * lane : 128 * lane + 128]
 
         loop(8, widen)
         for c in range(OWN):
@@ -206,19 +228,21 @@
                 t32[2 + lane, at, :] = tim[:, 128 * lane : 128 * lane + 128]
 
         def second(m):
-            at = pl.ds(128 * m, 128)
+            at = pl.ds(pl.multiple_of(128 * m, 128), 128)
             left = jnp.concatenate([t32[lane, at] for lane in range(4)], 1).astype(BF)
             dst[at] = jnp.dot(left, dfa[...], preferred_element_type=F32).astype(BF)
-
-        loop(8, second)
+            if then is not None:
+                then(m)
+
+        ring_z(second)
 
     def filter_at(m):
         at = pl.ds(8 * m, 8)
         return fr[at, 0].reshape(128, TOK).astype(F32), fr[at, 1].reshape(128, TOK).astype(F32)
 
-    def inverse(src, conj, dst):
+    def inverse(i, src, conj, dst, there):
         def first(m):
-            at = pl.ds(128 * m, 128)
+            at = pl.ds(pl.multiple_of(128 * m, 128), 128)
             sre, sim = src[at, 0:TOK].astype(F32), src[at, TOK:].astype(F32)
             fre, fim = filter_at(m)
             if conj:
@@ -241,10 +265,11 @@
                 s32[lane, at, :] = o[:, 128 * lane : 128 * lane + 128]
 
         def narrow(m):
-            wide = jnp.concatenate([s32[lane, pl.ds(128 * m, 128)] for lane in range(2)], 1)
+            wide = jnp.concatenate([s32[lane, pl.ds(pl.multiple_of(128 * m, 128), 128)] for lane in range(2)], 1)
             dst[pl.ds(8 * m, 8)] = wide.astype(BF).reshape(8, OWN, TOK)
-
-        loop(8, narrow)
+            send_home(i, dst, there, m)
+
+        ring_z(narrow)
 
     def back_at(src, c):
         return src[pl.ds(8 * c, 8)].reshape(128, TOK).astype(F32).T
@@ -255,12 +280,23 @@
     half_far = remote(cotg.at[0, t], cotg.at[0, t], ts.at[1], tr.at[1], tp=far)
     half_beside = remote(cots, cotg.at[1, t], ts.at[2], tr.at[2], seq=beside)
     half_across = remote(cots, cotg.at[1, t], ts.at[3], tr.at[3], seq=beside, tp=far)
-    send_all(0, xs, xr)
+    for d in row:
+        pl.semaphore_signal(row_sem, inc=1, device_id={"seq": d}, device_id_type=MESH)
     for copy in (half_sib, half_far, half_beside, half_across):
         copy.start()
+    for one in loads[1:3]:
+        one.wait()
+    loop(4, mix)
+    pl.semaphore_wait(row_sem, len(row))
+    pl.semaphore_signal(side_sem, inc=1, device_id={"seq": beside}, device_id_type=MESH)
+    loop(4, lambda c: mix(c + 4))
+    pl.semaphore_wait(side_sem, 1)
+    send_owners(0, xs, xr)
     zwait(0)
     zstart(1)
     xstart(1)
+    for one in loads[9:]:
+        one.wait()
     loads[3].wait()
 
     def turn_filter(c):
@@ -280,7 +316,7 @@
     xpass(1)
     zwait(3)
     xstart(4)
-    send_all(1, fs, fr)
+    send_owners(1, fs, fr)
     xpass(2)
     arrived = []
     for i, (tok, blk) in enumerate(((0, far), (1, t), (1, far))):
@@ -298,8 +334,7 @@
         ref = cotg.at[tok, blk]
         remote(ref, ref, ts.at[i], tr.at[i], tp=sib).wait_recv()
     wait_all(1, fs, fr)
-    inverse(spec, False, cs)
-    send_all(2, cs, cr)
+    inverse(2, spec, False, cs, cr)
     for k in range(5):
         xwait(k)
 
@@ -334,7 +369,7 @@
         grad_copy(n).wait_recv()
         turn_grad(2 * n)
         turn_grad(2 * n + 1)
-    send_all(3, gcs, gcr)
+        send_owners(3, gcs, gcr, 16 * n, 16)
 
     wait_all(2, cs, cr)
 
@@ -363,21 +398,18 @@
 
     out_blocks(0)
 
-    wait_all(3, gcs, gcr)
-    forward(gcr, gspec)
-
     def grad_filter(m):
-        at = pl.ds(128 * m, 128)
+        at = pl.ds(pl.multiple_of(128 * m, 128), 128)
         xre, xim = spec[at, 0:TOK].astype(F32), spec[at, TOK:].astype(F32)
         gre, gim = gspec[at, 0:TOK].astype(F32), gspec[at, TOK:].astype(F32)
         scale = 1.0 / LENGTH
         gfs[pl.ds(8 * m, 8), 0] = ((xre * gre + xim * gim) * scale).astype(BF).reshape(8, OWN, TOK)
         gfs[pl.ds(8 * m, 8), 1] = ((xre * gim - xim * gre) * scale).astype(BF).reshape(8, OWN, TOK)
-
-    loop(8, grad_filter)
-    send_all(4, gfs, gfr)
-    inverse(gspec, True, gms)
-    send_all(5, gms, gmr)
+        send_home(4, gfs, gfr, m)
+
+    wait_all(3, gcs, gcr)
+    forward(gcr, gspec, grad_filter)
+    inverse(5, gspec, True, gms, gmr)
 
     gat_copy.wait_recv()
     out_blocks(1)
@@ -436,8 +468,8 @@
     out[...] = out_in[...]
     gq[...] = gq_in[...]
     for p in range(2):
-        gf[p] = gfr[:, p].reshape(128, TOK).astype(F32).T
-    y = gmr[...].reshape(128, TOK).astype(F32).T
+        gf[p] = gfr[:, p].reshape(-1, TOK).astype(F32).T
+    y = gmr[...].reshape(-1, TOK).astype(F32).T
     gk[...] = (y * values[...].astype(F32)).astype(BF)
     gv[...] = (y * keys[...].astype(F32)).astype(BF)
 
@@ -446,7 +478,6 @@
     wt = weight.T
     filt = filter_spectrum.reshape(2, TOK, CH)
     anywhere = pl.BlockSpec(memory_space=pl.ANY)
-    vmem = pl.BlockSpec(memory_space=pltpu.VMEM)
     flat = jax.ShapeDtypeStruct((TOK, CH), BF)
     blocks = pltpu.VMEM((NS, OWN, TOK), BF)
     pairs = pltpu.VMEM((NS, 2, OWN, TOK), BF)
@@ -457,9 +488,15 @@
     out, gq, gfr, gmr = pl.pallas_call(
         kernel,
         out_shape=(flat, flat, pairs_out, blocks_out),
-        in_specs=[anywhere] * 6 + [vmem] * 6,
+        in_specs=[anywhere] * 12,
         out_specs=(anywhere,) * 4,
         scratch_shapes=[
+            pltpu.VMEM((2 * NS, NS), BF),
+            pltpu.VMEM((NS, 2 * NS), BF),
+            pltpu.VMEM((2 * TOK, 2 * TOK), BF),
+            pltpu.VMEM((2 * TOK, 2 * TOK), BF),
+            pltpu.VMEM((NS, TOK), F32),
+            pltpu.VMEM((NS, TOK), F32),
             whole, whole, whole,
             pltpu.VMEM((2, 4, TOK, 512), BF),
             pltpu.VMEM((TOK, 512), BF),
@@ -480,7 +517,8 @@
             pltpu.VMEM((2, 2, TOK, 512), BF),
             pltpu.VMEM((3, TOK, 512), BF),
             pltpu.VMEM((2, TOK, CH), BF),
-            dma((9,)), dma((2,)), dma((6,)), dma((6,)), dma((6,)),
+            pltpu.SemaphoreType.REGULAR, pltpu.SemaphoreType.REGULAR,
+            dma((15,)), dma((2,)), dma((6,)), dma((6,)), dma((6,)),
             dma((2, 4)), dma((2, 4)), dma((8, 2)), dma((8, 2)), dma((8, 2)), dma((8, 2)),
             dma((11,)), dma((11,)), dma((4,)), dma((4,)), dma((4,)), dma((4,)),
         ],
@@ -488,20 +526,20 @@
             collective_id=0, has_side_effects=True, vmem_limit_bytes=56 * 1024 * 1024
         ),
     )(keys, values, queries, cotangent, filt, wt, *tables())
-    lane = pl.BlockSpec((TOK, 128), lambda c: (0, c))
+    lane = pl.BlockSpec((TOK, CH // 2), lambda c: (0, c))
     out, gq, gk, gv, gf = pl.pallas_call(
         finish,
-        grid=(8,),
+        grid=(2,),
         out_shape=(flat, flat, flat, flat, jax.ShapeDtypeStruct((2, TOK, CH), F32)),
         in_specs=[
             lane,
             lane,
-            pl.BlockSpec((8, 2, OWN, TOK), lambda c: (c, 0, 0, 0)),
-            pl.BlockSpec((8, OWN, TOK), lambda c: (c, 0, 0)),
+            pl.BlockSpec((NS // 2, 2, OWN, TOK), lambda c: (c, 0, 0, 0)),
+            pl.BlockSpec((NS // 2, OWN, TOK), lambda c: (c, 0, 0)),
             lane,
             lane,
         ],
-        out_specs=(lane, lane, lane, lane, pl.BlockSpec((2, TOK, 128), lambda c: (0, 0, c))),
+        out_specs=(lane, lane, lane, lane, pl.BlockSpec((2, TOK, CH // 2), lambda c: (0, 0, c))),
         compiler_params=pltpu.CompilerParams(vmem_limit_bytes=56 * 1024 * 1024),
     )(out, gq, gfr, gmr, keys, values)
     return out, gq, gk, gv, gf.reshape(2, 1, TOK, CH)

time: 152 us -> 140 us (0.921)
  Pallas kernels: 151 us -> 138 us
    pallas_call x1, Pallas kernels: 144 us -> 134 us  [shards(): pl.pallas_call(kernel, out_shape=(flat, flat, pairs_out, blocks_out), in_...]
    pallas_call x1, Pallas kernels: 6.68 us -> 3.71 us  [shards(): pl.pallas_call(finish, grid=(2,), out_shape=(flat, flat, flat, flat, jax....]
where the time goes in v3:
time: 140 us; the launch traced here: 139 us
  Pallas kernels  138 us (99%)
    pallas_call x1, Pallas kernels, shards(): pl.pallas_call(kernel, out_shape=(flat, flat, pairs_out, blocks_out), in_...  134 us
    pallas_call x1, Pallas kernels, shards(): pl.pallas_call(finish, grid=(2,), out_shape=(flat, flat, flat, flat, jax....  3.71 us

profile of v3, /device:TPU:8, one launch (start us, length us, event | category | flops | bytes accessed | tf_op | source)
XLA Modules:
  0.0 138.7 jit_solution(10417890431731271177)
XLA Ops:
  0.6 134.4 %shard_map.155 = (bf16[256,1024]{1,0:T(8,128)(2,1)}, bf16[256,1024]{1,0:T(8,128)(2,1)}, bf16[64,2,16,256]{3,2,1,0:T(8,128)(2,1)}, bf16[64,16,256]{2,1,0:T(8,128)(2,1)}) custom-call(bf16[256,1024]{1,0:T(8,128)(2,1)} %keys.3, bf16[256,1024]{1,0:T(8,128)(2,1)} %values.3, bf16[256,1024]{1,0:T(8,128)(2,1)} %queries.1, bf16[256,1024]{1,0:T(8,128)(2,1)} %cot.1, ...), custom_call_target="tpu_custom_call" | custom-call | tf_op jit(solution)/shard_map/pallas_call | solution.py:488
  135.0 3.7 %shard_map.156 = (bf16[256,1024]{1,0:T(8,128)(2,1)}, bf16[256,1024]{1,0:T(8,128)(2,1)}, bf16[256,1024]{1,0:T(8,128)(2,1)}, bf16[256,1024]{1,0:T(8,128)(2,1)}, f32[2,256,1024]{2,1,0:T(8,128)}) custom-call(bf16[256,1024]{1,0:T(8,128)(2,1)} %get-tuple-element.14.out_in, bf16[256,1024]{1,0:T(8,128)(2,1)} %get-tuple-element.15.gq_in, ...), custom_call_target="tpu_custom_call" | custom-call | tf_op jit(solution)/shard_map/pallas_call | solution.py:530

commit v4 on v3

--- a/solution.py
+++ b/solution.py
@@ -103,7 +103,7 @@
             body(i)
             return carry
 
-        lax.fori_loop(0, n, step, 0)
+        lax.fori_loop(0, n, step, 0, unroll=4)
 
     def mix(c):
         at = lanes(c)
@@ -150,7 +150,8 @@
         loop(NR, one)
 
     def ring_z(body):
-        loop(NZ, lambda k: body(lax.rem(z + k, NZ)))
+        for k in (0, 4, 1, 7, 2, 6, 3, 5):
+            body(lax.rem(z + k, NZ))
 
     def wait_all(i, src, dst):
         remote(src.at[pl.ds(0, NS - 1)], dst.at[pl.ds(0, NS - 1)], a2s.at[i], a2r.at[i], seq=s).wait_recv()
@@ -310,13 +311,13 @@
     xstart(2)
     xpass(0)
     loop(4, lambda c: turn_filter(c + 4))
+    send_owners(1, fs, fr)
     zwait(2)
     zstart(3)
     xstart(3)
     xpass(1)
     zwait(3)
     xstart(4)
-    send_owners(1, fs, fr)
     xpass(2)
     arrived = []
     for i, (tok, blk) in enumerate(((0, far), (1, t), (1, far))):

time: 140 us -> 138 us (0.986); the launches traced: 139 us -> 138 us
  no operation moved by 1% of the time
where the time goes in v4:
time: 138 us
  Pallas kernels  138 us (100%)
    pallas_call x1, Pallas kernels, shards(): pl.pallas_call(kernel, out_shape=(flat, flat, pairs_out, blocks_out), in_...  134 us
    pallas_call x1, Pallas kernels, shards(): pl.pallas_call(finish, grid=(2,), out_shape=(flat, flat, flat, flat, jax....  3.71 us

profile of v4, /device:TPU:8, one launch (start us, length us, event | category | flops | bytes accessed | tf_op | source)
XLA Modules:
  0.0 138.2 jit_solution(1770723438176407417)
XLA Ops:
  0.6 133.9 %shard_map.155 = (bf16[256,1024]{1,0:T(8,128)(2,1)}, bf16[256,1024]{1,0:T(8,128)(2,1)}, bf16[64,2,16,256]{3,2,1,0:T(8,128)(2,1)}, bf16[64,16,256]{2,1,0:T(8,128)(2,1)}) custom-call(bf16[256,1024]{1,0:T(8,128)(2,1)} %keys.3, bf16[256,1024]{1,0:T(8,128)(2,1)} %values.3, bf16[256,1024]{1,0:T(8,128)(2,1)} %queries.1, bf16[256,1024]{1,0:T(8,128)(2,1)} %cot.1, ...), custom_call_target="tpu_custom_call" | custom-call | tf_op jit(solution)/shard_map/pallas_call | solution.py:489
  134.5 3.7 %shard_map.156 = (bf16[256,1024]{1,0:T(8,128)(2,1)}, bf16[256,1024]{1,0:T(8,128)(2,1)}, bf16[256,1024]{1,0:T(8,128)(2,1)}, bf16[256,1024]{1,0:T(8,128)(2,1)}, f32[2,256,1024]{2,1,0:T(8,128)}) custom-call(bf16[256,1024]{1,0:T(8,128)(2,1)} %get-tuple-element.14.out_in, bf16[256,1024]{1,0:T(8,128)(2,1)} %get-tuple-element.15.gq_in, ...), custom_call_target="tpu_custom_call" | custom-call | tf_op jit(solution)/shard_map/pallas_call | solution.py:531
